TPU v7x, 128 devices: a whole 4x4x4 slice. The times are simulated.
128 devices in a mesh: ctx: 32 (over x, z, core), fsdp: 4 (over y).
Axes of the slice: x: 4, y: 4, z: 4, core: 2. Of those that a mesh axis runs over, the one named last changes fastest.
Arguments:
- tokens: bfloat16 [8, 4096, 1280], P('fsdp', 'ctx'), may hold values from -6 to 6
- segment_ids: int32 [8, 4096], P('fsdp', 'ctx'), may hold values from 0 to 3, as said below
- cotangent: bfloat16 [8, 4096, 1280], P('fsdp', 'ctx'), may hold values from -6 to 6
- attn_in: bfloat16 [1280, 3840], P('fsdp'), may hold values from -0.15625 to 0.15625
- attn_out: bfloat16 [1280, 1280], P('fsdp'), may hold values from -1.25 to 1.25
- ffn_in: bfloat16 [1280, 1280], P('fsdp'), may hold values from -0.15625 to 0.15625
- ffn_out: bfloat16 [1280, 1280], P('fsdp'), may hold values from -0.15625 to 0.15625
- gain_attn: bfloat16 [1280], P('fsdp'), may hold values from 0.099609375 to 1.8984375
- gain_ffn: bfloat16 [1280], P('fsdp'), may hold values from 0.099609375 to 1.8984375
- query_scale: bfloat16 [80], P('fsdp'), may hold values from -3 to 3
Outputs:
- outputs: bfloat16 [8, 4096, 1280], P('fsdp', 'ctx')
- input_grad: float32 [8, 4096, 1280], P('fsdp', 'ctx')
- grad_attn_in: float32 [1280, 3840], P('fsdp')
- grad_attn_out: float32 [1280, 1280], P('fsdp')
- grad_ffn_in: float32 [1280, 1280], P('fsdp')
- grad_ffn_out: float32 [1280, 1280], P('fsdp')
- grad_gain_attn: float32 [1280], P('fsdp')
- grad_gain_ffn: float32 [1280], P('fsdp')
- grad_query_scale: float32 [80], P('fsdp')
Inputs may be any that keep to these rules, and one draw needn't show every extreme that they name: `segment_ids`: ids start at 0 at each sequence's first position and never fall, rising by at most one from a position to the next; a document is a run of equal ids. On each index of fsdp one of its 2 sequences is a single document; every other sequence has exactly 3 document starts after its first position, at positions drawn uniformly without repeats.
All inputs are finite; a program needn't handle non-finite values.
Results may differ from a plain program's by a relative error of at most 0.038.
Values may be sent and summed in bfloat16 or wider, within the bound.
No kernel may reach another device: no remote copies, remote signals or barrier semaphores. Data moves between devices by JAX's collectives and lax.ppermute only.
A program may use at most 320 MiB of HBM per device.

v0:
```python
import math

import jax
import jax.numpy as jnp
from jax import lax
from jax.sharding import PartitionSpec as P

HEADS = 16
HD = 80


EPS = 1e-06
QCONST = 1.442695041
NEG = -1e30


def shortened(value):
    return jax.tree.map(lambda a: a.astype(jnp.bfloat16) if a.dtype == jnp.float32 else a, value)


def norm_rows(values, gain):
    scale = lax.rsqrt(jnp.mean(values * values, -1, keepdims=True) + EPS)
    return (values * scale * gain, scale)


def norm_back(values, scale, gain, grad):
    shaped = grad * gain
    inner = jnp.mean(shaped * values, -1, keepdims=True)
    return (
        scale * shaped - values * scale * scale * scale * inner,
        jnp.sum(grad * values * scale, 0),
    )


def allowed_pairs(query_pos, query_seg, key_pos, key_seg):
    return ((query_seg[:, None] == key_seg[None, :]) & (key_pos[None, :] <= query_pos[:, None]))[
        None
    ]


def in_blocks(pieces, carry, inner):
    length = pieces[0].shape[0]
    width = math.gcd(length, 1024)
    count = length // width
    shaped = tuple((piece.reshape((count, width) + piece.shape[1:]) for piece in pieces))

    def advance(state, block):
        held, index = state
        return ((inner(held, block, index * width), index + 1), None)

    result, unused = lax.scan(advance, (carry, jnp.int32(0)), shaped)
    return result[0]


def split_heads(block):
    return block.reshape(block.shape[0], HEADS, HD)


def reduce_end(grads):
    shares = (
        lax.psum_scatter(
            grads[0].astype(jnp.bfloat16), "fsdp", scatter_dimension=0, tiled=True
        ).astype(jnp.float32),
        lax.psum_scatter(
            grads[1].astype(jnp.bfloat16), "fsdp", scatter_dimension=0, tiled=True
        ).astype(jnp.float32),
        lax.psum_scatter(
            grads[2].astype(jnp.bfloat16), "fsdp", scatter_dimension=0, tiled=True
        ).astype(jnp.float32),
        lax.psum_scatter(
            grads[3].astype(jnp.bfloat16), "fsdp", scatter_dimension=0, tiled=True
        ).astype(jnp.float32),
        lax.psum_scatter(
            grads[4].astype(jnp.bfloat16), "fsdp", scatter_dimension=0, tiled=True
        ).astype(jnp.float32),
        lax.psum_scatter(
            grads[5].astype(jnp.bfloat16), "fsdp", scatter_dimension=0, tiled=True
        ).astype(jnp.float32),
        lax.psum_scatter(
            grads[6].astype(jnp.bfloat16), "fsdp", scatter_dimension=0, tiled=True
        ).astype(jnp.float32),
    )
    return jax.tree.map(lambda part: part.astype(jnp.float32), lax.psum(shortened(shares), "ctx"))


def local(
    tokens,
    segment_ids,
    cotangent,
    attn_in,
    attn_out,
    ffn_in,
    ffn_out,
    gain_attn,
    gain_ffn,
    query_scale,
):
    batches, length, width = tokens.shape
    groups = lax.axis_size("fsdp")
    seq_length = length * lax.axis_size("ctx")
    all_segments = lax.all_gather(segment_ids, "ctx", axis=1, tiled=True)
    own_pos = lax.axis_index("ctx") * length + jnp.arange(length, dtype=jnp.int32)
    shapes = [
        (attn_in.shape[0] * groups, attn_in.shape[1]),
        (attn_out.shape[0] * groups, attn_out.shape[1]),
        (ffn_in.shape[0] * groups, ffn_in.shape[1]),
        (ffn_out.shape[0] * groups, ffn_out.shape[1]),
        (gain_attn.shape[0] * groups,),
        (gain_ffn.shape[0] * groups,),
        (query_scale.shape[0] * groups,),
    ]
    totals = tuple((jnp.zeros(shape, jnp.float32) for shape in shapes))
    shared = tuple((jnp.zeros((shape[0] // groups,) + shape[1:], jnp.float32) for shape in shapes))
    outputs = []
    input_grads = []
    for batch in range(batches):
        w_qkv, w_out, w_up, w_down, gain_one, gain_two, scale_raw = (
            lax.all_gather(attn_in, "fsdp", axis=0, tiled=True),
            lax.all_gather(attn_out, "fsdp", axis=0, tiled=True),
            lax.all_gather(ffn_in, "fsdp", axis=0, tiled=True),
            lax.all_gather(ffn_out, "fsdp", axis=0, tiled=True),
            lax.all_gather(gain_attn, "fsdp", axis=0, tiled=True),
            lax.all_gather(gain_ffn, "fsdp", axis=0, tiled=True),
            lax.all_gather(query_scale, "fsdp", axis=0, tiled=True),
        )
        gain_one = gain_one.astype(jnp.float32)
        gain_two = gain_two.astype(jnp.float32)
        scale_raw = scale_raw.astype(jnp.float32)
        factor = jax.nn.softplus(scale_raw) * (QCONST / math.sqrt(HD))
        inputs = tokens[batch].astype(jnp.float32)
        own_seg = segment_ids[batch]
        seq_seg = all_segments[batch]
        normed, first_scale = norm_rows(inputs, gain_one)
        normed_low = normed.astype(jnp.bfloat16)
        project = jnp.dot(normed_low, w_qkv, preferred_element_type=jnp.float32)
        query_raw = split_heads(project[:, :width])
        queries = (query_raw * factor).astype(jnp.bfloat16)
        keys_flat = project[:, width : 2 * width].astype(jnp.bfloat16)
        values_flat = project[:, 2 * width :].astype(jnp.bfloat16)

        def forward_block(state, block, start):
            best, total, accum = state
            key_heads = split_heads(block[0])
            value_heads = split_heads(block[1])
            count = key_heads.shape[0]
            key_pos = start + jnp.arange(count, dtype=jnp.int32)
            key_seg = lax.dynamic_slice_in_dim(seq_seg, start, count)
            mask = allowed_pairs(own_pos, own_seg, key_pos, key_seg)
            scores = jnp.where(
                mask,
                jnp.einsum("qhd,khd->hqk", queries, key_heads, preferred_element_type=jnp.float32),
                NEG,
            )
            newest = jnp.maximum(best, jnp.max(scores, -1))
            weights = jnp.where(mask, jnp.exp(scores - newest[..., None]), 0.0)
            decay = jnp.exp(best - newest)
            total = total * decay + jnp.sum(weights, -1)
            accum = accum * decay[..., None] + jnp.einsum(
                "hqk,khd->hqd",
                weights.astype(jnp.bfloat16),
                value_heads,
                preferred_element_type=jnp.float32,
            )
            return (newest, total, accum)

        start_state = (
            jnp.full((HEADS, length), NEG, jnp.float32),
            jnp.zeros((HEADS, length), jnp.float32),
            jnp.zeros((HEADS, length, HD), jnp.float32),
        )
        best, total, accum = in_blocks(
            (
                lax.all_gather(keys_flat, "ctx", axis=0, tiled=True),
                lax.all_gather(values_flat, "ctx", axis=0, tiled=True),
            ),
            start_state,
            forward_block,
        )
        log_total = best + jnp.log(total)
        attended_rows = (accum / total[..., None]).transpose(1, 0, 2).reshape(length, width)
        attended_low = attended_rows.astype(jnp.bfloat16)
        middle = inputs + jnp.dot(attended_low, w_out, preferred_element_type=jnp.float32)
        normed_two, second_scale = norm_rows(middle, gain_two)
        normed_two_low = normed_two.astype(jnp.bfloat16)
        hidden_pre = jnp.dot(normed_two_low, w_up, preferred_element_type=jnp.float32)
        hidden_low = jax.nn.silu(hidden_pre).astype(jnp.bfloat16)
        result = middle + jnp.dot(hidden_low, w_down, preferred_element_type=jnp.float32)
        outputs.append(result.astype(jnp.bfloat16))
        upstream = cotangent[batch]
        grad_down = jnp.einsum(
            "tf,td->fd", hidden_low, upstream, preferred_element_type=jnp.float32
        )
        grad_hidden = jnp.einsum("td,fd->tf", upstream, w_down, preferred_element_type=jnp.float32)
        gate_value = jax.nn.sigmoid(hidden_pre)
        grad_pre = (grad_hidden * gate_value * (1.0 + hidden_pre * (1.0 - gate_value))).astype(
            jnp.bfloat16
        )
        grad_up = jnp.einsum(
            "td,tf->df", normed_two_low, grad_pre, preferred_element_type=jnp.float32
        )
        grad_normed_two = jnp.einsum(
            "tf,df->td", grad_pre, w_up, preferred_element_type=jnp.float32
        )
        middle_part, grad_gain_two = norm_back(middle, second_scale, gain_two, grad_normed_two)
        grad_middle = upstream.astype(jnp.float32) + middle_part
        grad_branch = grad_middle.astype(jnp.bfloat16)
        grad_outw = jnp.einsum(
            "td,te->de", attended_low, grad_branch, preferred_element_type=jnp.float32
        )
        grad_att = jnp.einsum(
            "te,de->td", grad_branch, w_out, preferred_element_type=jnp.float32
        ).astype(jnp.bfloat16)
        grad_heads = split_heads(grad_att)
        delta = jnp.sum(split_heads(grad_att.astype(jnp.float32) * attended_rows), -1).T

        def query_terms(block, start):
            key_heads = split_heads(block[0])
            value_heads = split_heads(block[1])
            count = key_heads.shape[0]
            key_pos = start + jnp.arange(count, dtype=jnp.int32)
            key_seg = lax.dynamic_slice_in_dim(seq_seg, start, count)
            mask = allowed_pairs(own_pos, own_seg, key_pos, key_seg)
            scores = jnp.where(
                mask,
                jnp.einsum("qhd,khd->hqk", queries, key_heads, preferred_element_type=jnp.float32),
                NEG,
            )
            probs = jnp.where(mask, jnp.exp(scores - log_total[..., None]), 0.0)
            grad_probs = jnp.einsum(
                "qhd,khd->hqk", grad_heads, value_heads, preferred_element_type=jnp.float32
            )
            grad_scores = (probs * (grad_probs - delta[..., None])).astype(jnp.bfloat16)
            return (probs, grad_scores, key_heads, count)

        zero_query = jnp.zeros((HEADS, length, HD), jnp.float32)

        def backward_block(state, block, start):
            query_grad, buffer = state
            probs, grad_scores, key_heads, count = query_terms(block, start)
            query_grad = query_grad + jnp.einsum(
                "hqk,khd->hqd", grad_scores, key_heads, preferred_element_type=jnp.float32
            )
            key_part = jnp.einsum(
                "hqk,qhd->khd", grad_scores, queries, preferred_element_type=jnp.float32
            ).reshape(count, width)
            value_part = jnp.einsum(
                "hqk,qhd->khd",
                probs.astype(jnp.bfloat16),
                grad_heads,
                preferred_element_type=jnp.float32,
            ).reshape(count, width)
            current = lax.dynamic_slice_in_dim(buffer, start, count, 0)
            buffer = lax.dynamic_update_slice_in_dim(
                buffer, current + jnp.concatenate([key_part, value_part], 1), start, 0
            )
            return (query_grad, buffer)

        query_grad, buffer = in_blocks(
            (
                lax.all_gather(keys_flat, "ctx", axis=0, tiled=True),
                lax.all_gather(values_flat, "ctx", axis=0, tiled=True),
            ),
            (zero_query, jnp.zeros((seq_length, 2 * width), jnp.float32)),
            backward_block,
        )
        own_grads = lax.psum_scatter(
            buffer.astype(jnp.bfloat16), "ctx", scatter_dimension=0, tiled=True
        ).astype(jnp.float32)
        key_grad = own_grads[:, :width]
        value_grad = own_grads[:, width:]
        query_rows = query_grad.transpose(1, 0, 2)
        grad_scale = (
            jnp.sum(query_rows * query_raw, (0, 1))
            * jax.nn.sigmoid(scale_raw)
            * (QCONST / math.sqrt(HD))
        )
        grad_project = jnp.concatenate(
            [(query_rows * factor).reshape(length, width), key_grad, value_grad], 1
        ).astype(jnp.bfloat16)
        grad_qkv = jnp.einsum(
            "td,te->de", normed_low, grad_project, preferred_element_type=jnp.float32
        )
        grad_normed_one = jnp.einsum(
            "te,de->td", grad_project, w_qkv, preferred_element_type=jnp.float32
        )
        input_part, grad_gain_one = norm_back(inputs, first_scale, gain_one, grad_normed_one)
        input_grads.append(grad_middle + input_part)
        terms = (grad_qkv, grad_outw, grad_up, grad_down, grad_gain_one, grad_gain_two, grad_scale)
        totals = jax.tree.map(jnp.add, totals, terms)
    shared = reduce_end(totals)
    return (jnp.stack(outputs), jnp.stack(input_grads)) + tuple(shared)


def solution(mesh):
    placed = (
        P("fsdp", "ctx", None),
        P("fsdp", "ctx"),
        P("fsdp", "ctx", None),
        P("fsdp", None),
        P("fsdp", None),
        P("fsdp", None),
        P("fsdp", None),
        P("fsdp"),
        P("fsdp"),
        P("fsdp"),
    )
    return jax.shard_map(
        local,
        mesh=mesh,
        in_specs=placed,
        out_specs=(
            P("fsdp", "ctx", None),
            P("fsdp", "ctx", None),
            P("fsdp", None),
            P("fsdp", None),
            P("fsdp", None),
            P("fsdp", None),
            P("fsdp"),
            P("fsdp"),
            P("fsdp"),
        ),
        check_vma=False,
    )
```

profile of v0, /device:TPU:6, one launch (start us, length us, event | category | flops | bytes accessed | tf_op | source)
XLA Modules:
  0.0 1317.9 jit_solution(2679643050154259508)
XLA Ops:
  13.2 11.0 all-reduce.9
  25.6 81.7 %all-gather.9.cloned.1.call-done = bf16[1280,3840]{1,0:T(8,128)(2,1)} async-done(((bf16[320,3840]{1,0:T(8,128)(2,1)}), bf16[1280,3840]{1,0:T(8,128)(2,1)}) %all-gather.9.cloned.1.call-update) | async-done | bytes 9830416 | tf_op jit(solution)/shard_map/all_gather | solution.py:118
  107.3 5.5 fusion.145
  114.6 6.6 fusion.146
  124.8 24.3 %all_gather.47 = s32[2,4096]{1,0:T(2,128)S(1)} all-gather(s32[2,128]{1,0:T(2,128)S(1)} %copy-done.74), channel_id=1, replica_groups=mesh['ctx'=32,'fsdp'=4] {'ctx'}, dimensions={1}, use_global_device_ids=true | all-gather | bytes 33792 | tf_op jit(solution)/shard_map/all_gather | solution.py:101
  151.9 20.9 %all-gather.23.cloned.1.call-done = bf16[4096,1280]{1,0:T(8,128)(2,1)} async-done(((bf16[128,1280]{1,0:T(8,128)(2,1)}), bf16[4096,1280]{1,0:T(8,128)(2,1)}) %all-gather.23.cloned.1.call-update) | async-done | bytes 10485776 | tf_op jit(solution)/shard_map/all_gather | solution.py:174
  172.8 14.4 %copy.80 = bf16[4,1024,1280]{1,2,0:T(8,128)(2,1)} copy(bf16[4,1024,1280]{2,1,0:T(8,128)(2,1)} %bitcast.334) | data formatting | bytes 20971520
  187.2 45.9 %all-gather.21.cloned.1.call-done = bf16[4096,1280]{1,0:T(8,128)(2,1)} async-done(((bf16[128,1280]{1,0:T(8,128)(2,1)}), bf16[4096,1280]{1,0:T(8,128)(2,1)}) %all-gather.21.cloned.1.call-update) | async-done | bytes 10485776 | tf_op jit(solution)/shard_map/all_gather | solution.py:173
  233.1 14.4 %copy.79 = bf16[4,1024,1280]{1,2,0:T(8,128)(2,1)} copy(bf16[4,1024,1280]{2,1,0:T(8,128)(2,1)} %bitcast.335) | data formatting | bytes 20971520
  247.5 45.7 %all-gather.13.cloned.1.call-done = bf16[4096,1280]{1,0:T(8,128)(2,1)} async-done(((bf16[128,1280]{1,0:T(8,128)(2,1)}), bf16[4096,1280]{1,0:T(8,128)(2,1)}) %all-gather.13.cloned.1.call-update) | async-done | bytes 10485776 | tf_op jit(solution)/shard_map/all_gather | solution.py:174
  293.2 14.5 %copy.77 = bf16[4,1024,1280]{1,2,0:T(8,128)(2,1)} copy(bf16[4,1024,1280]{2,1,0:T(8,128)(2,1)} %bitcast.336) | data formatting | bytes 20971520
  307.6 45.1 %all-gather.11.cloned.1.call-done = bf16[4096,1280]{1,0:T(8,128)(2,1)} async-done(((bf16[128,1280]{1,0:T(8,128)(2,1)}), bf16[4096,1280]{1,0:T(8,128)(2,1)}) %all-gather.11.cloned.1.call-update) | async-done | bytes 10485776 | tf_op jit(solution)/shard_map/all_gather | solution.py:173
  352.7 14.6 %copy.76 = bf16[4,1024,1280]{1,2,0:T(8,128)(2,1)} copy(bf16[4,1024,1280]{2,1,0:T(8,128)(2,1)} %bitcast.337) | data formatting | bytes 20971520
  367.3 39.2 %while.68 = (s32[]{:T(128)}, f32[16,128]{1,0:T(8,128)S(1)}, f32[16,128]{1,0:T(8,128)S(1)}, f32[16,128,80]{1,2,0:T(8,128)S(1)}, s32[1,128]{1,0:T(1,128)S(1)}, /*i...) while((s32[]{:T(128)}, f32[16,128]{1,0:T(8,128)S(1)}, ...), condition=%wide.region_4.5_spmd.clone, body=%wide.region_1.4_spmd.clone.sunk | while | flops 692956288 | bytes 43210452 | solution.py:51
  407.5 43.4 %while.69 = (s32[]{:T(128)}, f32[16,128]{1,0:T(8,128)S(1)}, f32[16,128]{1,0:T(8,128)S(1)}, f32[16,128,80]{1,2,0:T(8,128)}, s32[1,128]{1,0:T(1,128)S(1)}, /*index...) while((s32[]{:T(128)}, f32[16,128]{1,0:T(8,128)S(1)}, ...), condition=%wide.region_10.11_spmd.clone, body=%wide.region_7.10_spmd.clone.sunk | while | flops 692956288 | bytes 48453388 | solution.py:51
  461.2 18.3 %all-gather.19.cloned.1.call-done = bf16[1280,1280]{1,0:T(8,128)(2,1)} async-done(((bf16[320,1280]{1,0:T(8,128)(2,1)}), bf16[1280,1280]{1,0:T(8,128)(2,1)}) %all-gather.19.cloned.1.call-update) | async-done | bytes 3276816 | tf_op jit(solution)/shard_map/all_gather | solution.py:121
  491.0 13.8 %broadcast.321.clone = f32[4096,2560]{0,1:T(8,128)} broadcast(f32[]{:T(128)} %constant.213.clone.1), dimensions={} | broadcast | bytes 41943044 | tf_op jit(solution)/shard_map/broadcast.12
  504.8 101.6 %while.71 = (s32[]{:T(128)}, f32[16,128,80]{1,2,0:T(8,128)S(1)}, f32[4096,2560]{0,1:T(8,128)}, s32[1,128]{1,0:T(1,128)S(1)}, s32[4096]{0:T(1024)S(1)}, /*index=5...) while((s32[]{:T(128)}, f32[16,128,80]{1,2,0:T(8,128)S(1)}, ...), condition=%wide.region_21.22_spmd.clone, body=%wide.region_20.21_spmd.clone.sunk | while | flops 1704658048 | bytes 101103336 | solution.py:51
  509.8 3.6 fusion.284
  518.4 12.0 fusion.287
  543.8 11.9 fusion.287
  569.2 11.9 fusion.287
  586.0 3.6 fusion.284
  594.6 11.8 fusion.287
  606.4 21.8 %convert_element_type.232 = bf16[4096,2560]{0,1:T(8,128)(2,1)} convert(f32[4096,2560]{0,1:T(8,128)} %get-tuple-element.760) | non-fusion elementwise | flops 10485760 | bytes 62914560 | tf_op jit(solution)/shard_map/convert_element_type | solution.py:267
  628.2 25.9 %copy.101 = bf16[4096,2560]{1,0:T(8,128)(2,1)} copy(bf16[4096,2560]{0,1:T(8,128)(2,1)} %convert_element_type.232) | data formatting | bytes 41943040
  663.3 18.7 %broadcast.321.clone.1 = f32[4096,2560]{0,1:T(8,128)} broadcast(f32[]{:T(128)} %constant.213.clone.1), dimensions={} | broadcast | bytes 41943044 | tf_op jit(solution)/shard_map/broadcast.12
  682.0 106.6 %while.70 = (s32[]{:T(128)}, f32[16,128,80]{1,2,0:T(8,128)S(1)}, f32[4096,2560]{0,1:T(8,128)}, s32[1,128]{1,0:T(1,128)S(1)}, s32[4096]{0:T(1024)}, /*index=5*/bf...) while((s32[]{:T(128)}, f32[16,128,80]{1,2,0:T(8,128)S(1)}, ...), condition=%wide.region_15.16_spmd.clone, body=%wide.region_14.15_spmd.clone.sunk | while | flops 1704658048 | bytes 101103336 | solution.py:51
  683.1 3.7 constant_dynamic-slice_fusion.14
  696.8 12.3 fusion.272
  710.2 4.1 constant_dynamic-slice_fusion.14
  724.2 12.2 fusion.272
  750.6 11.9 fusion.272
  776.8 11.9 fusion.272
  788.7 21.6 %convert_element_type.226 = bf16[4096,2560]{0,1:T(8,128)(2,1)} convert(f32[4096,2560]{0,1:T(8,128)} %get-tuple-element.757) | non-fusion elementwise | flops 10485760 | bytes 62914560 | tf_op jit(solution)/shard_map/convert_element_type | solution.py:267
  810.2 25.9 %copy.99 = bf16[4096,2560]{1,0:T(8,128)(2,1)} copy(bf16[4096,2560]{0,1:T(8,128)(2,1)} %convert_element_type.226) | data formatting | bytes 41943040
  856.8 106.7 %reduce-scatter.19.cloned.1.call-done = bf16[128,2560]{1,0:T(8,128)(2,1)} async-done(((bf16[4096,2560]{1,0:T(8,128)(2,1)}), bf16[128,2560]{1,0:T(8,128)(2,1)}) %reduce-scatter.19.cloned.1.call-update) | async-done | bytes 655376
  964.9 9.6 fusion.106
  974.5 11.1 add_convert_fusion
  993.8 11.0 reduce-scatter.15.cloned.1.call-done
  1004.8 41.9 %reduce-scatter.13.cloned.1.call-done = bf16[320,1280]{1,0:T(8,128)(2,1)} async-done(((bf16[1280,1280]{1,0:T(8,128)(2,1)}), bf16[320,1280]{1,0:T(8,128)(2,1)}) %reduce-scatter.13.cloned.1.call-update) | async-done | bytes 819216 | tf_op jit(solution)/shard_map/reduce_scatter | solution.py:64
  1046.8 41.5 %reduce-scatter.17.cloned.1.call-done = bf16[320,1280]{1,0:T(8,128)(2,1)} async-done(((bf16[1280,1280]{1,0:T(8,128)(2,1)}), bf16[320,1280]{1,0:T(8,128)(2,1)}) %reduce-scatter.17.cloned.1.call-update) | async-done | bytes 819216 | tf_op jit(solution)/shard_map/reduce_scatter | solution.py:70
  1088.3 94.3 %reduce-scatter.11.cloned.1.call-done = bf16[320,3840]{1,0:T(8,128)(2,1)} async-done(((bf16[1280,3840]{1,0:T(8,128)(2,1)}), bf16[320,3840]{1,0:T(8,128)(2,1)}) %reduce-scatter.11.cloned.1.call-update) | async-done | bytes 2457616 | tf_op jit(solution)/shard_map/reduce_scatter | solution.py:61
  1182.6 7.2 fusion.105
  1189.9 8.2 fusion.96
  1198.1 8.8 all-reduce.8
  1207.1 54.2 %all-reduce.6 = (bf16[320]{0:T(512)(128)(2,1)S(1)}, bf16[320]{0:T(512)(128)(2,1)S(1)}, bf16[20]{0:T(256)(128)(2,1)S(1)}) all-reduce(bf16[320]{0:T(512)(128)(2,1)S(1)} %dynamic-slice.4, bf16[320]{0:T(512)(128)(2,1)S(1)} %dynamic-slice.6, bf16[20]{0:T(256)(128)(2,1)S(1)} %dynamic-slice.8), channel_id=1, replica_groups=mesh['ctx'=32,'fsdp'=4] {'ctx'}, use_global_device_ids=true, to_apply=%region_35.36 | all-reduce | flops 660 | bytes 2640 | tf_op jit(solution)/shard_map/psum | solution.py:83
  1265.7 35.5 %all-reduce.12.cloned.1.call-done = (bf16[320,3840]{1,0:T(8,128)(2,1)}, bf16[320,1280]{1,0:T(8,128)(2,1)}, bf16[320,1280]{1,0:T(8,128)(2,1)}, bf16[320,1280]{1,0:T(8,128)(2,1)}) async-done(((bf16[320,3840]{1,0:T(8,128)(2,1)}, bf16[320,1280]{1,0:T(8,128)(2,1)}, bf16[320,1280]{1,0:T(8,128)(2,1)}, bf16[320,1280]{1,0:T(8,128)(2,1)}), (bf16[320,3840]{1,0:T(8,128)(2,1)}, bf16[320,1280]{1,0:T(8,128)(2,1)}, ...) | async-done | bytes 4915216 | tf_op jit(solution)/shard_map/psum | solution.py:83
  (451 shorter events, 266.4 us)
Async XLA Ops:
  7.2 100.2 %all-gather.9.cloned.1.call-start = ((), (), s32[]{:S(2)}) async-start(), calls=%async_computation.6 | async-start | bytes 12288000 | tf_op jit(solution)/shard_map/all_gather | solution.py:118
  7.9 164.9 %all-gather.23.cloned.1.call-start = ((), (), s32[]{:S(2)}) async-start(), calls=%async_computation.13 | async-start | bytes 10813440 | tf_op jit(solution)/shard_map/all_gather | solution.py:174
  24.2 125.0 %copy-start.75 = (bf16[80]{0:T(256)(128)(2,1)}, bf16[80]{0:T(256)(128)(2,1)S(1)}, u32[]{:S(2)}) copy-start(bf16[80]{0:T(256)(128)(2,1)S(1)} %get-tuple-element.1160) | copy-start | bytes 484
  24.2 90.3 %copy-start.52 = (f32[1280]{0:T(1024)}, f32[1280]{0:T(1024)S(1)}, u32[]{:S(2)}) copy-start(f32[1280]{0:T(1024)S(1)} %convert_element_type.204) | copy-start | bytes 15364
  25.6 87.3 %copy-start.66 = (f32[128]{0:T(128)}, f32[128]{0:T(128)S(1)}, u32[]{:S(2)}) copy-start(f32[128]{0:T(128)S(1)} %get-tuple-element.1214) | copy-start | bytes 1540
  25.6 89.0 %copy-start.64 = (f32[128]{0:T(128)}, f32[128]{0:T(128)S(1)}, u32[]{:S(2)}) copy-start(f32[128]{0:T(128)S(1)} %get-tuple-element.1215) | copy-start | bytes 1540
  113.7 119.3 %all-gather.21.cloned.1.call-start = ((), (), s32[]{:S(2)}) async-start(), calls=%async_computation.12 | async-start | bytes 10813440 | tf_op jit(solution)/shard_map/all_gather | solution.py:173
  114.5 178.7 %all-gather.13.cloned.1.call-start = ((), (), s32[]{:S(2)}) async-start(), calls=%async_computation.8 | async-start | bytes 10813440 | tf_op jit(solution)/shard_map/all_gather | solution.py:174
  114.6 10.3 copy-start.74
  122.1 230.6 %all-gather.11.cloned.1.call-start = ((), (), s32[]{:S(2)}) async-start(), calls=%async_computation.7 | async-start | bytes 10813440 | tf_op jit(solution)/shard_map/all_gather | solution.py:173
  122.7 330.5 %all-gather.15.cloned.1.call-start = ((), (), s32[]{:S(2)}) async-start(), calls=%async_computation.9 | async-start | bytes 4096000 | tf_op jit(solution)/shard_map/all_gather | solution.py:119
  123.2 335.1 %all-gather.17.cloned.1.call-start = ((), (), s32[]{:S(2)}) async-start(), calls=%async_computation.10 | async-start | bytes 4096000 | tf_op jit(solution)/shard_map/all_gather | solution.py:120
  124.0 355.5 %all-gather.19.cloned.1.call-start = ((), (), s32[]{:S(2)}) async-start(), calls=%async_computation.11 | async-start | bytes 4096000 | tf_op jit(solution)/shard_map/all_gather | solution.py:121
  124.7 730.5 %reduce-scatter.21.cloned.1.call-start = ((), (), s32[]{:S(2)}) async-start(), calls=%async_computation.19 | async-start | bytes 21626880
  149.2 38.0 %copy-start.72 = (f32[80]{0:T(128)}, f32[80]{0:T(128)S(1)}, u32[]{:S(2)}) copy-start(f32[80]{0:T(128)S(1)} %fusion.132) | copy-start | bytes 964
  150.1 37.1 %copy-start.27 = (f32[128,1280]{0,1:T(8,128)}, f32[128,1280]{0,1:T(8,128)S(1)}, u32[]{:S(2)}) copy-start(f32[128,1280]{0,1:T(8,128)S(1)} %copy.78) | copy-start | bytes 1966084
  151.7 35.5 %copy-start.26 = (f32[128,1280]{0,1:T(8,128)}, f32[128,1280]{0,1:T(8,128)S(1)}, u32[]{:S(2)}) copy-start(f32[128,1280]{0,1:T(8,128)S(1)} %copy.75) | copy-start | bytes 1966084
  352.7 14.6 %copy-start.50 = (f32[16,128,80]{1,2,0:T(8,128)S(1)}, f32[16,128,80]{1,2,0:T(8,128)}, u32[]{:S(2)}) copy-start(f32[16,128,80]{1,2,0:T(8,128)} %custom-call.2) | copy-start | bytes 1966084
  406.6 49.4 %copy-start.56 = (f32[16,128]{1,0:T(8,128)}, f32[16,128]{1,0:T(8,128)S(1)}, u32[]{:S(2)}) copy-start(f32[16,128]{1,0:T(8,128)S(1)} %get-tuple-element.752) | copy-start | bytes 24580
  407.4 45.8 %copy-start.13 = (bf16[2,128,1280]{2,1,0:T(8,128)(2,1)S(1)}, bf16[2,128,1280]{2,1,0:T(8,128)(2,1)}, u32[]{:S(2)}) copy-start(bf16[2,128,1280]{2,1,0:T(8,128)(2,1)} %param.18) | copy-start | bytes 1966084
  456.0 32.1 %copy-start.15 = (f32[128,1280]{1,0:T(8,128)}, f32[128,1280]{1,0:T(8,128)S(1)}, u32[]{:S(2)}) copy-start(f32[128,1280]{1,0:T(8,128)S(1)} %get-tuple-element.1203) | copy-start | bytes 1966084
  456.0 32.0 %copy-start.70 = (f32[128]{0:T(128)}, f32[128]{0:T(128)S(1)}, u32[]{:S(2)}) copy-start(f32[128]{0:T(128)S(1)} %add_rsqrt_fusion) | copy-start | bytes 1540
  458.3 29.8 %copy-start.10 = (f32[128,1280]{1,0:T(8,128)}, f32[128,1280]{1,0:T(8,128)S(1)}, u32[]{:S(2)}) copy-start(f32[128,1280]{1,0:T(8,128)S(1)} %get-tuple-element.1207) | copy-start | bytes 1966084
  458.3 29.8 %copy-start.68 = (f32[128]{0:T(128)}, f32[128]{0:T(128)S(1)}, u32[]{:S(2)}) copy-start(f32[128]{0:T(128)S(1)} %add_rsqrt_fusion.2) | copy-start | bytes 1540
  461.2 22.9 %copy-start.35 = (f32[128,1280]{1,0:T(8,128)}, f32[128,1280]{1,0:T(8,128)S(1)}, u32[]{:S(2)}) copy-start(f32[128,1280]{1,0:T(8,128)S(1)} %fusion.139) | copy-start | bytes 1966084
  489.3 15.5 %copy-start.23 = (f32[128,1280]{1,0:T(8,128)}, f32[128,1280]{1,0:T(8,128)S(1)}, u32[]{:S(2)}) copy-start(f32[128,1280]{1,0:T(8,128)S(1)} %get-tuple-element.1185) | copy-start | bytes 1966084
  491.0 13.8 %copy-start.6 = (f32[16,128,80]{1,2,0:T(8,128)S(1)}, f32[16,128,80]{1,2,0:T(8,128)}, u32[]{:S(2)}) copy-start(f32[16,128,80]{1,2,0:T(8,128)} %custom-call.7) | copy-start | bytes 1966084
  606.4 21.8 %copy-start.7 = (f32[16,128,80]{1,2,0:T(8,128)}, f32[16,128,80]{1,2,0:T(8,128)S(1)}, u32[]{:S(2)}) copy-start(f32[16,128,80]{1,2,0:T(8,128)S(1)} %get-tuple-element.759) | copy-start | bytes 1966084
  654.1 9.1 copy-start.47
  654.2 309.3 %reduce-scatter.19.cloned.1.call-start = ((), (), s32[]{:S(2)}) async-start(), calls=%async_computation.18 | async-start | bytes 21626880
  663.3 18.7 %copy-start.1 = (bf16[128,16,80]{0,2,1:T(8,128)(2,1)S(1)}, bf16[128,16,80]{0,2,1:T(8,128)(2,1)}, u32[]{:S(2)}) copy-start(bf16[128,16,80]{0,2,1:T(8,128)(2,1)} %copy-done) | copy-start | bytes 983044
  663.3 18.7 %copy-start.9 = (f32[16,128,80]{1,2,0:T(8,128)S(1)}, f32[16,128,80]{1,2,0:T(8,128)}, u32[]{:S(2)}) copy-start(f32[16,128,80]{1,2,0:T(8,128)} %custom-call.6) | copy-start | bytes 1966084
  663.3 18.7 %copy-start.58 = (bf16[128,1280]{0,1:T(8,128)(2,1)S(1)}, bf16[128,1280]{0,1:T(8,128)(2,1)}, u32[]{:S(2)}) copy-start(bf16[128,1280]{0,1:T(8,128)(2,1)} %copy.81) | copy-start | bytes 983044
  663.3 18.7 %copy-start.61 = (s32[1,128]{1,0:T(1,128)S(1)}, s32[1,128]{1,0:T(1,128)}, u32[]{:S(2)}) copy-start(s32[1,128]{1,0:T(1,128)} %copy-done.60) | copy-start | bytes 1540
  836.2 168.6 %reduce-scatter.15.cloned.1.call-start = ((), (), s32[]{:S(2)}) async-start(), calls=%async_computation.16 | async-start | bytes 4096000 | tf_op jit(solution)/shard_map/reduce_scatter | solution.py:67
  841.3 205.5 %reduce-scatter.13.cloned.1.call-start = ((), (), s32[]{:S(2)}) async-start(), calls=%async_computation.15 | async-start | bytes 4096000 | tf_op jit(solution)/shard_map/reduce_scatter | solution.py:64
  846.3 242.0 %reduce-scatter.17.cloned.1.call-start = ((), (), s32[]{:S(2)}) async-start(), calls=%async_computation.17 | async-start | bytes 4096000 | tf_op jit(solution)/shard_map/reduce_scatter | solution.py:70
  851.4 113.5 %copy-start.14 = (bf16[2,128,1280]{2,1,0:T(8,128)(2,1)S(1)}, bf16[2,128,1280]{2,1,0:T(8,128)(2,1)}, u32[]{:S(2)}) copy-start(bf16[2,128,1280]{2,1,0:T(8,128)(2,1)} %param.18) | copy-start | bytes 1966084
  851.4 113.5 %copy-start.53 = (f32[1280]{0:T(1024)S(1)}, f32[1280]{0:T(1024)}, u32[]{:S(2)}) copy-start(f32[1280]{0:T(1024)} %copy-done.52) | copy-start | bytes 15364
  851.4 113.5 %copy-start.65 = (f32[128]{0:T(128)S(1)}, f32[128]{0:T(128)}, u32[]{:S(2)}) copy-start(f32[128]{0:T(128)} %copy-done.64) | copy-start | bytes 1540
  851.4 331.1 %reduce-scatter.11.cloned.1.call-start = ((), (), s32[]{:S(2)}) async-start(), calls=%async_computation.14 | async-start | bytes 12288000 | tf_op jit(solution)/shard_map/reduce_scatter | solution.py:61
  853.0 121.5 %copy-start.31 = (bf16[128,16,80]{0,2,1:T(8,128)(2,1)}, bf16[128,16,80]{0,2,1:T(8,128)(2,1)S(1)}, u32[]{:S(2)}) copy-start(bf16[128,16,80]{0,2,1:T(8,128)(2,1)S(1)} %get-tuple-element.1187) | copy-start | bytes 983044
  964.9 9.6 copy-start.33
  964.9 9.6 copy-start.67
  985.7 315.6 %all-reduce.12.cloned.1.call-start = ((), (), s32[]{:S(2)}) async-start(), calls=%async_computation.20 | async-start | bytes 9830400 | tf_op jit(solution)/shard_map/psum | solution.py:83
  990.2 192.4 %copy-start.32 = (bf16[128,16,80]{0,2,1:T(8,128)(2,1)S(1)}, bf16[128,16,80]{0,2,1:T(8,128)(2,1)}, u32[]{:S(2)}) copy-start(bf16[128,16,80]{0,2,1:T(8,128)(2,1)} %copy-done.31) | copy-start | bytes 983044
  1189.8 73.2 %copy-start.22 = (f32[128,1280]{1,0:T(8,128)S(1)}, f32[128,1280]{1,0:T(8,128)}, u32[]{:S(2)}) copy-start(f32[128,1280]{1,0:T(8,128)} %get-tuple-element.1184) | copy-start | bytes 1966084
  1189.8 73.2 %copy-start.25 = (f32[128,1280]{1,0:T(8,128)S(1)}, f32[128,1280]{1,0:T(8,128)}, u32[]{:S(2)}) copy-start(f32[128,1280]{1,0:T(8,128)} %copy-done.23) | copy-start | bytes 1966084
  (51 other events, 147.0 us)
Sparse Core Ops, SparseCore 0:
  9.7 97.6 all-gather.8
  113.9 58.8 all-gather.22
  175.6 57.3 all-gather.20
  235.7 57.3 all-gather.12
  295.3 57.3 all-gather.10
  354.2 40.1 all-gather.14
  396.0 40.8 all-gather.16
  438.6 40.8 all-gather.18
  654.3 128.2 reduce-scatter.20
  836.3 127.1 reduce-scatter.18
  965.9 38.8 reduce-scatter.14
  1007.7 39.0 reduce-scatter.12
  1049.2 39.0 reduce-scatter.16
  1090.6 91.9 reduce-scatter.10
  1186.8 114.3 all-reduce.11
where the time goes:
time: 1330 us; the launch traced here: 1320 us
  waiting for transfers between devices  593 us (45%)
  local copies, waits for them, and re-layouts  220 us (17%)
  matrix products  202 us (15%)
  other arithmetic  184 us (14%)
  blocking collectives  98.3 us (7%)
  between operations  18 us (1%)
    unnamed x170, local copies, waits for them, and re-layouts  119 us
    unnamed x17, waiting for transfers between devices  111 us
    dynamic_update_slice x8, other arithmetic, backward_block(): lax.dynamic_update_slice_in_dim(buffer, current + jnp.concatenate([key_pa...  96 us
    reduce_scatter x1, waiting for transfers between devices, reduce_end(): lax.psum_scatter(grads[0].astype(jnp.bfloat16), 'fsdp', scatter_dimension...  94.3 us
    all_gather x2, waiting for transfers between devices, local(): lax.all_gather(keys_flat, 'ctx', axis=0, tiled=True)  90.9 us
    all_gather x1, waiting for transfers between devices, local(): lax.all_gather(attn_in, 'fsdp', axis=0, tiled=True)  81.7 us
    all_gather x2, waiting for transfers between devices, local(): lax.all_gather(values_flat, 'ctx', axis=0, tiled=True)  66.6 us
    psum x1, blocking collectives, reduce_end(): lax.psum(shortened(shares), 'ctx')  54.2 us
  transfers between devices with their start and end apart: 15, of which 12 were waited for; matrix products, arithmetic and copies ran while one was open for 31% of the time, Pallas kernels for 0%

commit v1 on v0

v1 whole, which is shorter than its diff:
```python
import math

import jax
import jax.numpy as jnp
from jax import lax
from jax.experimental import pallas as pl
from jax.experimental.pallas import tpu as pltpu
from jax.sharding import Mesh
from jax.sharding import PartitionSpec as P

D = 1280
HEADS = 16
HD = 80
EPS = 1e-06
QCONST = 1.442695041
NEG = -1e30
F32 = jnp.float32
BF16 = jnp.bfloat16
VMEM_LIMIT = 56 * 1024 * 1024
CHIPS = ("x", "z")


def dot(a, b):
    return jnp.dot(a, b, preferred_element_type=F32)


def dot_nt(a, b):
    return lax.dot_general(a, b, (((1,), (1,)), ((), ())), preferred_element_type=F32)


def dot_tn(a, b):
    return lax.dot_general(a, b, (((0,), (0,)), ((), ())), preferred_element_type=F32)


def qkv_kernel(x_ref, gain_ref, wt_ref, wkv_ref, factor_ref, first_ref, qt_ref, raw_ref, k_ref, v_ref, kt_ref, vt_ref):
    x = x_ref[...].astype(F32)
    scale = lax.rsqrt(jnp.mean(x * x, -1, keepdims=True) + EPS)
    first = (x * scale * gain_ref[...]).astype(BF16)
    first_ref[...] = first
    projected = dot_nt(wt_ref[...], first)
    raw = projected[:HD]
    queries = (raw * factor_ref[...]).astype(BF16)
    keys = projected[HD : 2 * HD].astype(BF16)
    values = projected[2 * HD :].astype(BF16)
    rows = dot(first, wkv_ref[...]).astype(BF16)
    for s in range(2):
        part = slice(128 * s, 128 * s + 128)
        qt_ref[s] = queries[:, part]
        raw_ref[s] = raw[:, part]
        kt_ref[s] = keys[:, part]
        vt_ref[s] = values[:, part]
        k_ref[s] = rows[part, :128]
        v_ref[s] = rows[part, 128:]


def qkv_call(gathered, gain, wt, wkv, factor):
    whole = lambda *shape: pl.BlockSpec(shape, lambda g: (0,) * len(shape))
    wide = pl.BlockSpec((2, HD, 128), lambda g: (0, 0, g))
    tall = pl.BlockSpec((2, 128, 128), lambda g: (0, g, 0))
    return pl.pallas_call(
        qkv_kernel,
        grid=(16,),
        in_specs=[
            pl.BlockSpec((256, D), lambda g: (g, 0)),
            whole(1, D),
            whole(3 * HD, D),
            whole(D, 256),
            whole(HD, 1),
        ],
        out_specs=[pl.BlockSpec((256, D), lambda g: (g, 0)), wide, wide, tall, tall, wide, wide],
        out_shape=[
            jax.ShapeDtypeStruct((4096, D), BF16),
            jax.ShapeDtypeStruct((2, HD, 2048), BF16),
            jax.ShapeDtypeStruct((2, HD, 2048), F32),
            jax.ShapeDtypeStruct((2, 2048, 128), BF16),
            jax.ShapeDtypeStruct((2, 2048, 128), BF16),
            jax.ShapeDtypeStruct((2, HD, 2048), BF16),
            jax.ShapeDtypeStruct((2, HD, 2048), BF16),
        ],
        compiler_params=pltpu.CompilerParams(vmem_limit_bytes=VMEM_LIMIT),
        name="qkv",
    )(gathered, gain, wt, wkv, factor)


def tile_positions():
    row = lax.broadcasted_iota(jnp.int32, (256, 256), 0)
    column = lax.broadcasted_iota(jnp.int32, (1, 256), 1)
    spread = lambda r: r + jnp.where(r >= 128, 128, 0)
    return spread(row), spread(column)


def forward_kernel(bounds, qt_ref, ko_ref, kx_ref, vto_ref, vtx_ref, start_ref, out_ref, low_ref, lse_ref):
    core = bounds[32]
    key_base, query_base = tile_positions()

    def query_tile(index, unused):
        s, t = index // 8, index % 8
        columns = pl.ds(pl.multiple_of(t * 256, 256), 256)
        queries = qt_ref[s, :, columns]
        query_pos = query_base + (512 * t + 128 * core)
        starts = start_ref[s, :, columns]

        def score(keys_ref, block, which, masked):
            rows = pl.ds(pl.multiple_of(block * 256, 256), 256)
            scores = dot(keys_ref[s, rows, :HD], queries)
            if masked:
                shift = 512 * block + 128 * which
                mask = (key_base <= query_pos - shift) & (key_base >= starts - shift)
                scores = jnp.where(mask, scores, NEG)
            return scores

        def tile(block, masked, state):
            best, total, accum = state
            one = score(ko_ref, block, core, masked)
            two = score(kx_ref, block, 1 - core, masked)
            newest = jnp.maximum(
                best, jnp.max(jnp.maximum(one, two), 0, keepdims=True)
            )
            one = jnp.exp(one - newest)
            two = jnp.exp(two - newest)
            decay = jnp.exp(best - newest)
            columns = pl.ds(pl.multiple_of(block * 256, 256), 256)
            total = total * decay + jnp.sum(one + two, 0, keepdims=True)
            accum = (
                accum * decay
                + dot(vto_ref[s, :, columns], one.astype(BF16))
                + dot(vtx_ref[s, :, columns], two.astype(BF16))
            )
            return newest, total, accum

        state = (jnp.full((1, 256), NEG, F32), jnp.zeros((1, 256), F32), jnp.zeros((HD, 256), F32))
        state = tile(t, True, state)
        low, high = bounds[index], bounds[16 + index]
        state = lax.fori_loop(high, t, lambda b, st: tile(b, False, st), state)
        best, total, accum = lax.fori_loop(low, high, lambda b, st: tile(b, True, st), state)
        result = accum / total
        out_ref[s, :, columns] = result
        lse_ref[s, :, columns] = best + jnp.log(total)
        lanes = pl.ds(pl.multiple_of(s * 128, 128), 128)
        result = result.astype(BF16)
        low_ref[2 * t, :, lanes] = result[:, :128]
        low_ref[2 * t + 1, :, lanes] = result[:, 128:]
        return unused

    lax.fori_loop(0, 16, query_tile, 0)


def tall(wide):
    return jnp.concatenate([wide, jnp.zeros((128 - HD, 256), F32)], 0).T.astype(BF16)


def backward_kernel(
    bounds, qt_ref, raw_ref, ko_ref, kx_ref, vo_ref, vx_ref, kto_ref, ktx_ref, start_ref, out_ref, lse_ref, grad_ref, factor_ref,
    dq_ref, scale_ref, dko_ref, dvo_ref, dkx_ref, dvx_ref, dk_acc, dv_acc,
):
    core = bounds[32]
    key_base, query_base = tile_positions()
    for ref in (dko_ref, dvo_ref, dk_acc, dv_acc):
        ref[...] = jnp.zeros_like(ref)
    scale_ref[...] = jnp.zeros_like(scale_ref)

    def query_tile(index, unused):
        s, t = index // 8, index % 8
        columns = pl.ds(pl.multiple_of(t * 256, 256), 256)
        queries = qt_ref[s, :, columns]
        query_rows = tall(queries.astype(F32))
        query_pos = query_base + (512 * t + 128 * core)
        starts = start_ref[s, :, columns]
        lse = lse_ref[s, :, columns]
        lanes = pl.ds(pl.multiple_of(s * 128, 128), 128)
        grads = jnp.concatenate([grad_ref[2 * t, :, lanes], grad_ref[2 * t + 1, :, lanes]], 1)
        wide = grads.astype(F32)
        grad_rows = tall(wide)
        delta = jnp.sum(wide * out_ref[s, :, columns], 0, keepdims=True)

        def tile(block, masked, dq):
            rows = pl.ds(pl.multiple_of(block * 256, 256), 256)
            for k_ref, v_ref, kt_ref, dk_ref, dv_ref, which in (
                (ko_ref, vo_ref, kto_ref, dko_ref, dvo_ref, core),
                (kx_ref, vx_ref, ktx_ref, dk_acc, dv_acc, 1 - core),
            ):
                probs = jnp.exp(dot(k_ref[s, rows, :HD], queries) - lse)
                if masked:
                    shift = 512 * block + 128 * which
                    mask = (key_base <= query_pos - shift) & (key_base >= starts - shift)
                    probs = jnp.where(mask, probs, 0.0)
                dprobs = dot(v_ref[s, rows, :HD], grads)
                dscores = (probs * (dprobs - delta)).astype(BF16)
                dv_ref[s, rows, :] += dot(probs.astype(BF16), grad_rows)
                dk_ref[s, rows, :] += dot(dscores, query_rows)
                dq = dq + dot(kt_ref[s, :, rows], dscores)
            return dq

        dq = tile(t, True, jnp.zeros((HD, 256), F32))
        low, high = bounds[index], bounds[16 + index]
        dq = lax.fori_loop(high, t, lambda b, st: tile(b, False, st), dq)
        dq = lax.fori_loop(low, high, lambda b, st: tile(b, True, st), dq)
        scale_ref[...] += dq * raw_ref[s, :, columns]
        result = (dq * factor_ref[...]).astype(BF16)
        dq_ref[2 * t, :, lanes] = result[:, :128]
        dq_ref[2 * t + 1, :, lanes] = result[:, 128:]
        return unused

    lax.fori_loop(0, 16, query_tile, 0)
    dkx_ref[...] = dk_acc[...].astype(BF16)
    dvx_ref[...] = dv_acc[...].astype(BF16)


def whole_call(kernel, inputs, out_shape, scratch, name, cost):
    vmem = pl.BlockSpec(memory_space=pltpu.VMEM)
    return pl.pallas_call(
        kernel,
        in_specs=[pl.BlockSpec(memory_space=pltpu.SMEM)] + [vmem] * (len(inputs) - 1),
        out_specs=[vmem] * len(out_shape),
        out_shape=out_shape,
        scratch_shapes=scratch,
        compiler_params=pltpu.CompilerParams(vmem_limit_bytes=VMEM_LIMIT),
        cost_estimate=pl.CostEstimate(flops=cost, bytes_accessed=16 << 20, transcendentals=8 << 20),
        name=name,
    )(*inputs)


def weight_kernel(dq_ref, dko_ref, dkr_ref, dvo_ref, dvr_ref, first_ref, grad_ref, weight_ref, accum):
    g = pl.program_id(0)

    @pl.when(g == 0)
    def _():
        accum[...] = jnp.zeros_like(accum)

    grad_ref[0, :HD] = dq_ref[0]
    for base, own_ref, far_ref in ((HD, dko_ref, dkr_ref), (2 * HD, dvo_ref, dvr_ref)):
        for s in range(2):
            total = own_ref[s] + far_ref[s].astype(F32)
            grad_ref[0, base : base + HD, 128 * s : 128 * s + 128] = total.T[:HD].astype(BF16)
    accum[...] += dot(grad_ref[0], first_ref[...])

    @pl.when(g == 15)
    def _():
        weight_ref[...] = jnp.concatenate([accum[...], jnp.zeros((16, D), F32)], 0).T


def weight_call(dq, dko, dkr, dvo, dvr, first):
    tall = pl.BlockSpec((2, 128, 128), lambda g: (0, g, 0))
    return pl.pallas_call(
        weight_kernel,
        grid=(16,),
        in_specs=[
            pl.BlockSpec((1, HD, 256), lambda g: (g, 0, 0)),
            tall,
            tall,
            tall,
            tall,
            pl.BlockSpec((256, D), lambda g: (g, 0)),
        ],
        out_specs=[
            pl.BlockSpec((1, 3 * HD, 256), lambda g: (g, 0, 0)),
            pl.BlockSpec((D, 256), lambda g: (0, 0)),
        ],
        out_shape=[
            jax.ShapeDtypeStruct((16, 3 * HD, 256), BF16),
            jax.ShapeDtypeStruct((D, 256), F32),
        ],
        scratch_shapes=[pltpu.VMEM((3 * HD, D), F32)],
        compiler_params=pltpu.CompilerParams(vmem_limit_bytes=VMEM_LIMIT),
        name="weight",
    )(dq, dko, dkr, dvo, dvr, first)


def assemble_kernel(zero_ref, one_ref, out_ref, scale_ref):
    total = jnp.zeros((8, 256), F32)
    for c, ref in enumerate((zero_ref, one_ref)):
        for h in range(HEADS):
            total = total + ref[h, 160:168].astype(F32)
        for part in range(3):
            lanes = slice(HD * part, HD * part + HD)
            out_ref[160 * c : 160 * c + 160, D * part : D * part + D] = jnp.concatenate(
                [ref[h, :160, lanes].astype(F32) for h in range(HEADS)], 1
            )
    scale_ref[...] = total


def assemble_call(zero, one):
    return pl.pallas_call(
        assemble_kernel,
        out_shape=[jax.ShapeDtypeStruct((320, 3 * D), F32), jax.ShapeDtypeStruct((8, 256), F32)],
        compiler_params=pltpu.CompilerParams(vmem_limit_bytes=VMEM_LIMIT),
        name="assemble",
    )(zero, one)


def other_core(value):
    return lax.ppermute(value, "core", [(0, 1), (1, 0)])


def scatter_sum_y(parts):
    y = lax.axis_index("y")
    piece = lambda step: lax.dynamic_index_in_dim(parts, (y + step) % 4, 0, keepdims=False)
    total = piece(0).astype(F32)
    for step in (1, 3, 2):
        pairs = [(i, (i + step) % 4) for i in range(4)]
        total = total + lax.ppermute(piece(step).astype(BF16), "y", pairs).astype(F32)
    return total


def gather_y(value):
    return lax.all_gather(value, "y", axis=0, tiled=True)


def gather_rows(value):
    rows = value.shape[0] // 2
    half = lax.dynamic_slice_in_dim(value, lax.axis_index("core") * rows, rows, 0)
    return lax.all_gather(half, ("y", "core"), axis=0, tiled=True)


def swap(value):
    return lax.all_to_all(value, CHIPS, 0, 0, tiled=True)


def norm_scale(values):
    return lax.rsqrt(jnp.mean(values * values, -1, keepdims=True) + EPS)


def norm_back(values, scale, gain, grad):
    shaped = grad * gain
    inner = jnp.mean(shaped * values, -1, keepdims=True)
    return scale * shaped - values * scale * scale * scale * inner


def local(tokens, segment_ids, cotangent, attn_in, attn_out, ffn_in, ffn_out, gain_attn, gain_ffn, query_scale):
    core = lax.axis_index("core")
    head = lax.axis_index("x") * 4 + lax.axis_index("z")
    inputs_low = tokens.reshape(256, D)
    upstream = cotangent.reshape(256, D)

    gathered = lax.all_gather(inputs_low, CHIPS, axis=0, tiled=True)

    mine = lax.dynamic_index_in_dim(attn_in.reshape(320, 3, HEADS, HD), head, 2, keepdims=False).reshape(320, 3 * HD)
    small = jnp.concatenate([gain_attn[:, None], gain_ffn[:, None], jnp.pad(query_scale, (0, 300))[:, None]], 1)
    small = gather_y(jnp.concatenate([mine, jnp.pad(small, ((0, 0), (0, 13)))], 1))
    head_weights = small[:, : 3 * HD]
    gain_one = small[:, 240].reshape(1, D).astype(F32)
    gain_two = small[:, 241].reshape(1, D).astype(F32)
    scale_raw = small[:, 242].reshape(4, 320)[:, :20].reshape(HD).astype(F32)
    factor = jax.nn.softplus(scale_raw) * (QCONST / math.sqrt(HD))
    factor_column = factor[:, None]
    w_out, w_up, w_down = gather_rows(attn_out), gather_rows(ffn_in), gather_rows(ffn_out)

    segments = lax.all_gather(segment_ids, ("x", "z", "core"), axis=1, tiled=True)
    begins = [jnp.sum((segments < k).astype(jnp.int32), 1, keepdims=True) for k in range(1, 4)]
    own_segments = lax.dynamic_index_in_dim(segments.reshape(2, 16, 2, 128), core, 2, keepdims=False).reshape(2, 2048)
    starts = jnp.zeros_like(own_segments)
    for k in range(1, 4):
        starts = jnp.where(own_segments == k, begins[k - 1], starts)
    by_tile = starts.reshape(2, 8, 256)
    low = by_tile[:, :, 0] // 512
    high = jnp.minimum((by_tile[:, :, 255] + 511) // 512, jnp.arange(8, dtype=jnp.int32)[None])
    high = jnp.maximum(low, high)
    bounds = jnp.concatenate([low.reshape(16), high.reshape(16), core[None].astype(jnp.int32)])
    starts = starts[:, None, :]

    blank = jnp.zeros((D, 128 - HD), BF16)
    head_kv = jnp.concatenate([head_weights[:, HD : 2 * HD], blank, head_weights[:, 2 * HD :], blank], 1)
    first, qt, raw, k_own, v_own, kt_own, vt_own = qkv_call(gathered, gain_one, head_weights.T, head_kv, factor_column)
    k_far, vt_far, v_far, kt_far = other_core(k_own), other_core(vt_own), other_core(v_own), other_core(kt_own)

    shape = jax.ShapeDtypeStruct
    attended, attended_low, lse = whole_call(
        forward_kernel,
        (bounds, qt, k_own, k_far, vt_own, vt_far, starts),
        [shape((2, HD, 2048), F32), shape((16, HD, 256), BF16), shape((2, 1, 2048), F32)],
        [],
        "attention",
        8 << 30,
    )
    attended_t = swap(attended_low).reshape(D, 256)

    inputs = inputs_low.astype(F32)
    middle = inputs + dot_tn(attended_t, w_out)
    second_scale = norm_scale(middle)
    second = (middle * second_scale * gain_two).astype(BF16)
    hidden_pre = dot(second, w_up)
    gate = jax.nn.sigmoid(hidden_pre)
    hidden = jax.nn.silu(hidden_pre).astype(BF16)
    grad_hidden = dot_nt(upstream, w_down)
    grad_pre = (grad_hidden * gate * (1.0 + hidden_pre * (1.0 - gate))).astype(BF16)
    grad_second = dot_nt(grad_pre, w_up)
    grad_middle = upstream.astype(F32) + norm_back(middle, second_scale, gain_two, grad_second)
    grad_branch = grad_middle.astype(BF16)
    grad_attended = dot_nt(w_out, grad_branch).astype(BF16).reshape(16, HD, 256)
    grad_attended, hidden, second, attended_t = lax.optimization_barrier((grad_attended, hidden, second, attended_t))
    grad_attended = swap(grad_attended)
    outputs = (middle + dot(hidden, w_down)).astype(BF16)

    def half_columns(which):
        cut = lambda value: lax.dynamic_slice_in_dim(value, which * 640, 640, 1)
        parts = [dot(attended_t, cut(grad_branch)), dot_tn(second, cut(grad_pre)), dot_tn(hidden, cut(upstream))]
        return jnp.concatenate([part.astype(BF16) for part in parts], 1)

    give = half_columns(1 - core)
    summed = (half_columns(core).astype(F32) + other_core(give).astype(F32)).astype(BF16)
    summed = lax.psum_scatter(summed, "y", scatter_dimension=0, tiled=True)

    dq, scale_terms, dk_own, dv_own, dk_far, dv_far = whole_call(
        backward_kernel,
        (bounds, qt, raw, k_own, k_far, v_own, v_far, kt_own, kt_far, starts, attended, lse, grad_attended, factor_column),
        [
            shape((16, HD, 256), BF16),
            shape((HD, 256), F32),
            shape((2, 2048, 128), F32),
            shape((2, 2048, 128), F32),
            shape((2, 2048, 128), BF16),
            shape((2, 2048, 128), BF16),
        ],
        [pltpu.VMEM((2, 2048, 128), F32), pltpu.VMEM((2, 2048, 128), F32)],
        "attention_back",
        20 << 30,
    )
    grad_project, head_grad = weight_call(dq, dk_own, other_core(dk_far), dv_own, other_core(dv_far), first)

    scale_part = jnp.sum(scale_terms, 1).reshape(4, 1, 20)
    scale_part = jnp.pad(scale_part, ((0, 0), (0, 7), (0, 236)))
    head_parts = head_grad.reshape(4, 2, 160, 256)
    keep = lax.dynamic_index_in_dim(head_parts, core, 1, keepdims=False)
    give = lax.dynamic_index_in_dim(head_parts, 1 - core, 1, keepdims=False)
    head_sum = keep + other_core(give.astype(BF16)).astype(F32)
    head_sum = scatter_sum_y(jnp.concatenate([head_sum, scale_part], 1))

    grad_project = swap(grad_project)
    w_qkv = gather_rows(attn_in)
    columns = grad_project.reshape(HEADS, 3, HD, 256).transpose(1, 0, 2, 3).reshape(3 * D, 256)
    grad_first = lax.dot_general(columns, w_qkv, (((0,), (1,)), ((), ())), preferred_element_type=F32)
    input_grad = grad_middle + norm_back(inputs, norm_scale(inputs), gain_one, grad_first)

    square_sum = jnp.sum(swap(summed.reshape(16, 20, 3 * 640)).astype(F32), 0).astype(BF16)
    squares = swap(jnp.broadcast_to(square_sum[None], (16, 20, 3 * 640))).reshape(320, 3 * 640)
    far_squares = other_core(squares)
    squares = jnp.where(core == 0, squares, far_squares), jnp.where(core == 0, far_squares, squares)
    grad_out, grad_up, grad_down = (
        jnp.concatenate([part[:, 640 * i : 640 * i + 640] for part in squares], 1).astype(F32) for i in range(3)
    )
    heads = swap(jnp.broadcast_to(head_sum.astype(BF16)[None], (16, 168, 256)))
    far_heads = other_core(heads)
    heads = jnp.where(core == 0, heads, far_heads), jnp.where(core == 0, far_heads, heads)
    grad_attn_in, scale_sum = assemble_call(*heads)
    own_gain = lambda value: value.astype(F32)
    grad_gain_one = jnp.sum(grad_attn_in * attn_in.astype(F32), 1) / own_gain(gain_attn)
    grad_gain_two = jnp.sum(grad_up * ffn_in.astype(F32), 1) / own_gain(gain_ffn)
    own_scale = query_scale.astype(F32)
    grad_scale = scale_sum[0, :20] * jax.nn.sigmoid(own_scale) * (QCONST / math.sqrt(HD))
    return (
        outputs.reshape(2, 128, D),
        input_grad.reshape(2, 128, D),
        grad_attn_in,
        grad_out,
        grad_up,
        grad_down,
        grad_gain_one,
        grad_gain_two,
        grad_scale,
    )


def solution(mesh):
    split = Mesh(mesh.devices.reshape(4, 4, 2, 4), ("x", "z", "core", "y"))
    rows = P("y", ("x", "z", "core"), None)
    weight = P("y", None)
    vector = P("y")
    return jax.shard_map(
        local,
        mesh=split,
        in_specs=(rows, P("y", ("x", "z", "core")), rows) + (weight,) * 4 + (vector,) * 3,
        out_specs=(rows, rows) + (weight,) * 4 + (vector,) * 3,
        check_vma=False,
    )
```

time: 1330 us -> 467 us (0.35)
  waiting for transfers between devices: 593 us -> 126 us
  local copies, waits for them, and re-layouts: 220 us -> 38.3 us
  matrix products: 202 us -> 32 us
  other arithmetic: 184 us -> 32.5 us
  Pallas kernels: 0 us -> 112 us
  starting transfers between devices: 1.18 us -> 41.1 us
  blocking collectives: 98.3 us -> 63 us
    all_gather x8 -> x5, waiting for transfers between devices: 258 us -> 45.1 us  [the longest x1 32.1 us: local(): gathered = lax.all_gather(inputs_low, CHIPS, axis=0, tiled=True)]
    reduce_scatter x4 -> x1, waiting for transfers between devices: 189 us -> 0.01 us  [local(): summed = lax.psum_scatter(summed, 'y', scatter_dimension=0, tiled=True)]
    dot_general x80 -> x13, matrix products: 202 us -> 32 us  [the longest x4 9.94 us: dot(): return jnp.dot(a, b, preferred_element_type=F32)]
    pallas_call x0 -> x5, Pallas kernels: none -> 112 us  [the longest x2 72.7 us: whole_call(): pl.pallas_call(kernel, in_specs=[pl.BlockSpec(memory_space=pltpu.SMEM)] +...]
    unnamed x17 -> x6, waiting for transfers between devices: 111 us -> 0.76 us
    unnamed x170 -> x60, local copies, waits for them, and re-layouts: 119 us -> 18.3 us
    dynamic_update_slice x8 -> x0, other arithmetic: 96 us -> none  [backward_block(): lax.dynamic_update_slice_in_dim(buffer, current + jnp.concatenate([key_pa...]
    all_to_all x0 -> x5, waiting for transfers between devices: none -> 59.2 us  [swap(): return lax.all_to_all(value, CHIPS, 0, 0, tiled=True)]
  transfers between devices with their start and end apart: 15 -> 24, of which waited for: 12 -> 15; matrix products, arithmetic and copies ran while one was open for 31% -> 15% of each run, Pallas kernels for 0% -> 24%
where the time goes in v1:
time: 467 us; the launch traced here: 459 us
  waiting for transfers between devices  126 us (27%)
  Pallas kernels  112 us (24%)
  blocking collectives  63 us (13%)
  starting transfers between devices  41.1 us (9%)
  local copies, waits for them, and re-layouts  38.3 us (8%)
  other arithmetic  32.5 us (7%)
  matrix products  32 us (7%)
  between operations  14.7 us (3%)
    pallas_call x2, Pallas kernels, whole_call(): pl.pallas_call(kernel, in_specs=[pl.BlockSpec(memory_space=pltpu.SMEM)] +...  72.7 us
    all_to_all x5, waiting for transfers between devices, swap(): return lax.all_to_all(value, CHIPS, 0, 0, tiled=True)  59.2 us
    all_to_all x5, starting transfers between devices, swap(): return lax.all_to_all(value, CHIPS, 0, 0, tiled=True)  33.4 us
    all_gather x1, waiting for transfers between devices, local(): gathered = lax.all_gather(inputs_low, CHIPS, axis=0, tiled=True)  32.1 us
    all_gather x1, blocking collectives, local(): lax.all_gather(segment_ids, ('x', 'z', 'core'), axis=1, tiled=True)  25.1 us
    all_to_all x1, blocking collectives, swap(): return lax.all_to_all(value, CHIPS, 0, 0, tiled=True)  24.1 us
    unnamed x60, local copies, waits for them, and re-layouts  18.3 us
    pallas_call x1, Pallas kernels, qkv_call(): pl.pallas_call(qkv_kernel, grid=(16,), in_specs=[pl.BlockSpec((256, D), l...  17.1 us
  transfers between devices with their start and end apart: 24, of which 15 were waited for; matrix products, arithmetic and copies ran while one was open for 15% of the time, Pallas kernels for 24%

profile of v1, /device:TPU:6, one launch (start us, length us, event | category | flops | bytes accessed | tf_op | source)
XLA Modules:
  0.0 459.2 jit_solution(4093926478935636606)
XLA Ops:
  11.1 25.1 %all_gather.21 = s32[2,4096]{1,0:T(2,128)S(1)} all-gather(s32[2,128]{1,0:T(2,128)S(1)} %copy-done.24), channel_id=1, replica_groups=mesh['x'=4,'z'=4,'core'=2,'y'=4] {'x','z','core'}, dimensions={1}, use_global_device_ids=true | all-gather | bytes 33792 | tf_op jit(solution)/shard_map/all_gather | solution.py:348
  36.6 4.4 copy.97
  42.2 13.8 %all_gather.23 = bf16[1280,256]{1,0:T(8,128)(2,1)S(1)} all-gather(bf16[320,256]{1,0:T(8,128)(2,1)S(1)} %fusion.21), channel_id=1, replica_groups=mesh['x'=4,'z'=4,'core'=2,'y'=4] {'y'}, dimensions={0}, use_global_device_ids=true | all-gather | bytes 819200 | tf_op jit(solution)/shard_map/all_gather | solution.py:306
  61.0 32.1 %all-gather.6.cloned.1.call-done.x_ref = bf16[4096,1280]{1,0:T(8,128)(2,1)} async-done(((bf16[256,1280]{1,0:T(8,128)(2,1)}), bf16[4096,1280]{1,0:T(8,128)(2,1)}) %all-gather.6.cloned.1.call-update) | async-done | bytes 10485776 | tf_op jit(solution)/shard_map/all_gather | solution.py:335
  93.2 17.1 %qkv.1 = (bf16[4096,1280]{1,0:T(8,128)(2,1)}, bf16[2,80,2048]{2,1,0:T(8,128)(2,1)}, f32[2,80,2048]{2,1,0:T(8,128)}, bf16[2,2048,128]{2,1,0:T(8,128)(2,1)}, bf16[...) custom-call(bf16[4096,1280]{1,0:T(8,128)(2,1)} %all-gather.6.cloned.1.call-done.x_ref, ...), custom_call_target="tpu_custom_call" | custom-call | tf_op jit(solution)/shard_map/qkv/pallas_call | solution.py:60
  112.7 1.6 collective-permute-done.1.vtx_ref
  115.5 30.3 %attention.1 = (f32[2,80,2048]{2,1,0:T(8,128)}, bf16[16,80,256]{2,1,0:T(8,128)(2,1)}, f32[2,1,2048]{2,1,0:T(1,128)}) custom-call(s32[33]{0:T(128)} %pad_add_fusion.bounds, bf16[2,80,2048]{2,1,0:T(8,128)(2,1)} %get-tuple-element.33.qt_ref, bf16[2,2048,128]{2,1,0:T(8,128)(2,1)} %get-tuple-element.34.ko_ref, bf16[2,2048,128]{2,1,0:T(8,128)(2,1)} %copy-done.27, ...), custom_call_target="tpu_custom_call" | custom-call | flops 8589934592 | bytes 16777216 | tf_op jit(solution)/shard_map/attention/pallas_call | solution.py:211
  145.8 5.9 %all-to-all-start = ((bf16[16,80,256]{2,1,0:T(8,128)(2,1)}), bf16[16,80,256]{2,1,0:T(8,128)(2,1)S(1)}, u32[]{:S(2)}, u32[]{:S(2)}) async-start(bf16[16,80,256]{2,1,0:T(8,128)(2,1)} %get-tuple-element.36), calls=%async_computation | async-start | bytes 1310720 | tf_op jit(solution)/shard_map/all_to_all | solution.py:316
  151.9 9.3 %all-to-all-done = bf16[16,80,256]{2,1,0:T(8,128)(2,1)S(1)} async-done(((bf16[16,80,256]{2,1,0:T(8,128)(2,1)}), bf16[16,80,256]{2,1,0:T(8,128)(2,1)S(1)}, u32[]{:S(2)}, u32[]{:S(2)}) %all-to-all-start) | async-done | bytes 655392 | tf_op jit(solution)/shard_map/all_to_all | solution.py:316
  161.3 3.4 multiply_reduce_fusion.4
  164.9 4.6 %multiply_convert_fusion = (bf16[256,1280]{0,1:T(8,128)(2,1)}, f32[256,1280]{0,1:T(8,128)}) fusion(bf16[256,1280]{1,0:T(8,128)(2,1)S(1)} %multiply_convert_fusion.1, bf16[1280,1280]{1,0:T(8,128)(2,1)} %all-gather.12.cloned.1.call-done), kind=kOutput, calls=%fused_computation.31 | convolution fusion | flops 840499200 | bytes 5898240 | tf_op jit(solution)/shard_map/dot_general | solution.py:24
  169.6 12.9 %all-gather.10.cloned.1.call-done = bf16[1280,1280]{1,0:T(8,128)(2,1)} async-done(((bf16[160,1280]{1,0:T(8,128)(2,1)}), bf16[1280,1280]{1,0:T(8,128)(2,1)}) %all-gather.10.cloned.1.call-update) | async-done | bytes 3276816 | tf_op jit(solution)/shard_map/all_gather | solution.py:312
  182.5 3.6 fusion.2
  187.9 1.5 copy-done.26
  189.3 1.9 convolution_convert_fusion.6
  193.6 2.5 pad_maximum_fusion
  196.4 1.9 convolution_convert_fusion.4
  200.2 4.5 collective-permute-done.11
  204.6 4.7 %add_convert_fusion = bf16[1280,1920]{0,1:T(8,128)(2,1)} fusion(bf16[1280,1920]{0,1:T(8,128)(2,1)} %collective-permute-done.11, bf16[1280,640]{0,1:T(8,128)(2,1)S(1)} %convolution_convert_fusion.4, bf16[1280,640]{0,1:T(8,128)(2,1)S(1)} %convolution_convert_fusion.1, bf16[1280,640]{0,1:T(8,128)(2,1)S(1)} %convolution_convert_fusion.5), kind=kLoop, calls=%fused_computation | loop fusion | flops 22118400 | bytes 14745600 | tf_op jit(solution)/shard_map/convert_element_type | solution.py:400
  209.3 7.8 %copy.118 = bf16[1280,1920]{1,0:T(8,128)(2,1)} copy(bf16[1280,1920]{0,1:T(8,128)(2,1)} %add_convert_fusion) | data formatting | bytes 9830400
  217.2 2.4 constant_dynamic-slice_fusion
  220.2 7.4 %all-to-all-start.1 = ((bf16[16,80,256]{2,1,0:T(8,128)(2,1)}), bf16[16,80,256]{2,1,0:T(8,128)(2,1)S(1)}, u32[]{:S(2)}, u32[]{:S(2)}) async-start(bf16[16,80,256]{2,1,0:T(8,128)(2,1)} %bitcast.8), calls=%async_computation.1 | async-start | bytes 1310720 | tf_op jit(solution)/shard_map/all_to_all | solution.py:316
  227.6 11.2 %all-to-all-done.1.grad_ref = bf16[16,80,256]{2,1,0:T(8,128)(2,1)S(1)} async-done(((bf16[16,80,256]{2,1,0:T(8,128)(2,1)}), bf16[16,80,256]{2,1,0:T(8,128)(2,1)S(1)}, u32[]{:S(2)}, u32[]{:S(2)}) %all-to-all-start.1) | async-done | bytes 655392 | tf_op jit(solution)/shard_map/all_to_all | solution.py:316
  239.6 42.4 %attention_back.1 = (bf16[16,80,256]{2,1,0:T(8,128)(2,1)}, f32[80,256]{1,0:T(8,128)}, f32[2,2048,128]{2,1,0:T(8,128)}, f32[2,2048,128]{2,1,0:T(8,128)}, bf16[2,2...) custom-call(s32[33]{0:T(128)} %pad_add_fusion.bounds, bf16[2,80,2048]{2,1,0:T(8,128)(2,1)} %get-tuple-element.33.qt_ref, ...), custom_call_target="tpu_custom_call" | custom-call | flops 21474836480 | bytes 16777216 | tf_op jit(solution)/shard_map/attention_back/pallas_call | solution.py:211
  282.5 2.5 collective-permute-done.4.dkr_ref
  285.0 3.0 collective-permute-done.5.dvr_ref
  288.0 16.4 %weight.1 = (bf16[16,240,256]{2,1,0:T(8,128)(2,1)}, f32[1280,256]{1,0:T(8,128)}) custom-call(bf16[16,80,256]{2,1,0:T(8,128)(2,1)} %get-tuple-element.44.dq_ref, f32[2,2048,128]{2,1,0:T(8,128)} %get-tuple-element.45.dko_ref, bf16[2,2048,128]{2,1,0:T(8,128)(2,1)} %collective-permute-done.4.dkr_ref, f32[2,2048,128]{2,1,0:T(8,128)} %get-tuple-element.47.dvo_ref, ...), custom_call_target="tpu_custom_call" | custom-call | tf_op jit(solution)/shard_map/weight/pallas_call | solution.py:244
  309.1 2.8 collective-permute-start.9
  312.0 2.3 collective-permute-start.8
  314.3 3.8 collective-permute-done.9
  318.1 3.3 collective-permute-done.8
  323.5 24.1 %all_to_all.30 = bf16[16,168,256]{2,1,0:T(8,128)(2,1)} all-to-all(bf16[16,168,256]{2,1,0:T(8,128)(2,1)S(1)} %broadcast_in_dim.79), channel_id=1, replica_groups=mesh['x'=4,'z'=4,'core'=2,'y'=4] {'x','z'}, dimensions={0} | all-to-all | bytes 2752512 | tf_op jit(solution)/shard_map/all_to_all | solution.py:316
  347.6 6.3 %all-to-all-start.2 = ((bf16[16,240,256]{2,1,0:T(8,128)(2,1)}), bf16[16,240,256]{2,1,0:T(8,128)(2,1)}, u32[]{:S(2)}, u32[]{:S(2)}) async-start(bf16[16,240,256]{2,1,0:T(8,128)(2,1)} %get-tuple-element.50), calls=%async_computation.2 | async-start | bytes 3932160 | tf_op jit(solution)/shard_map/all_to_all | solution.py:316
  354.0 2.3 reshape.309
  356.3 20.7 %all-to-all-done.2 = bf16[16,240,256]{2,1,0:T(8,128)(2,1)} async-done(((bf16[16,240,256]{2,1,0:T(8,128)(2,1)}), bf16[16,240,256]{2,1,0:T(8,128)(2,1)}, u32[]{:S(2)}, u32[]{:S(2)}) %all-to-all-start.2) | async-done | bytes 1966112 | tf_op jit(solution)/shard_map/all_to_all | solution.py:316
  377.0 7.0 %all-to-all-start.4 = ((bf16[16,20,1920]{2,1,0:T(8,128)(2,1)}), bf16[16,20,1920]{2,1,0:T(8,128)(2,1)}, u32[]{:S(2)}, u32[]{:S(2)}) async-start(bf16[16,20,1920]{2,1,0:T(8,128)(2,1)} %reshape.309), calls=%async_computation.4 | async-start | bytes 2949120 | tf_op jit(solution)/shard_map/all_to_all | solution.py:316
  384.3 4.0 fusion.3
  388.3 3.0 copy.113
  391.3 9.1 %all-to-all-done.4 = bf16[16,20,1920]{2,1,0:T(8,128)(2,1)} async-done(((bf16[16,20,1920]{2,1,0:T(8,128)(2,1)}), bf16[16,20,1920]{2,1,0:T(8,128)(2,1)}, u32[]{:S(2)}, u32[]{:S(2)}) %all-to-all-start.4) | async-done | bytes 1228832 | tf_op jit(solution)/shard_map/all_to_all | solution.py:316
  400.4 1.6 reduce_sum.110
  403.2 6.8 %all-to-all-start.5 = ((bf16[16,20,1920]{2,1,0:T(8,128)(2,1)}), bf16[16,20,1920]{2,1,0:T(8,128)(2,1)}, u32[]{:S(2)}, u32[]{:S(2)}) async-start(bf16[16,20,1920]{2,1,0:T(8,128)(2,1)} %broadcast_in_dim.80), calls=%async_computation.5 | async-start | bytes 2949120 | tf_op jit(solution)/shard_map/all_to_all | solution.py:316
  410.0 8.2 %fusion.9 = (f32[256]{0:T(256)S(1)}, f32[256,1280]{1,0:T(8,128)}) fusion(bf16[2,128,1280]{2,1,0:T(8,128)(2,1)S(1)} %copy-done.7, f32[1280]{0:T(1024)S(1)} %get-tuple-element.58, bf16[3840,256]{1,0:T(8,128)(2,1)} %bitcast.115, bf16[1280,3840]{1,0:T(8,128)(2,1)} %all-gather.14.cloned.1.call-done), kind=kOutput, calls=%fused_computation.29 | convolution fusion | flops 2517892864 | bytes 13768704 | tf_op jit(solution)/shard_map/dot_general | solution.py:431
  418.2 8.9 %all-to-all-done.5 = bf16[16,20,1920]{2,1,0:T(8,128)(2,1)} async-done(((bf16[16,20,1920]{2,1,0:T(8,128)(2,1)}), bf16[16,20,1920]{2,1,0:T(8,128)(2,1)}, u32[]{:S(2)}, u32[]{:S(2)}) %all-to-all-start.5) | async-done | bytes 1228832 | tf_op jit(solution)/shard_map/all_to_all | solution.py:316
  427.2 2.3 reshape.310
  429.5 3.3 fusion.8
  432.7 3.5 broadcast_select_fusion
  436.2 5.4 %assemble.1 = (f32[320,3840]{1,0:T(8,128)}, f32[8,256]{1,0:T(8,128)}) custom-call(bf16[16,168,256]{2,1,0:T(8,128)(2,1)} %get-tuple-element.69.zero_ref, bf16[16,168,256]{2,1,0:T(8,128)(2,1)} %get-tuple-element.68.one_ref), custom_call_target="tpu_custom_call" | custom-call | tf_op jit(solution)/shard_map/assemble/pallas_call | solution.py:283
  441.6 3.1 multiply_reduce_fusion
  (164 shorter events, 38.5 us)
Async XLA Ops:
  7.2 1.2 copy-start
  7.2 2.1 copy-start.17
  7.2 86.0 %all-gather.6.cloned.1.call-start = ((), (), s32[]{:S(2)}) async-start(), calls=%async_computation.7 | async-start | bytes 11141120 | tf_op jit(solution)/shard_map/all_gather | solution.py:335
  7.9 2.2 copy-start.20
  7.9 144.0 %all-gather.8.cloned.1.call-start = ((), (), s32[]{:S(2)}) async-start(), calls=%async_computation.8 | async-start | bytes 3686400 | tf_op jit(solution)/shard_map/all_gather | solution.py:312
  9.2 1.9 copy-start.24
  9.2 27.1 %copy-start.25 = (bf16[20]{0:T(256)(128)(2,1)S(1)}, bf16[20]{0:T(256)(128)(2,1)}, u32[]{:S(2)}) copy-start(bf16[20]{0:T(256)(128)(2,1)} %param.19) | copy-start | bytes 124
  9.2 27.2 %copy-start.23 = (bf16[320]{0:T(512)(128)(2,1)S(1)}, bf16[320]{0:T(512)(128)(2,1)}, u32[]{:S(2)}) copy-start(bf16[320]{0:T(512)(128)(2,1)} %param.18) | copy-start | bytes 1924
  9.2 27.2 %copy-start.22 = (bf16[320]{0:T(512)(128)(2,1)S(1)}, bf16[320]{0:T(512)(128)(2,1)}, u32[]{:S(2)}) copy-start(bf16[320]{0:T(512)(128)(2,1)} %param.17) | copy-start | bytes 1924
  9.2 155.7 %all-gather.12.cloned.1.call-start = ((), (), s32[]{:S(2)}) async-start(), calls=%async_computation.10 | async-start | bytes 3686400 | tf_op jit(solution)/shard_map/all_gather | solution.py:312
  10.1 172.3 %all-gather.10.cloned.1.call-start = ((), (), s32[]{:S(2)}) async-start(), calls=%async_computation.9 | async-start | bytes 3686400 | tf_op jit(solution)/shard_map/all_gather | solution.py:312
  110.3 4.0 collective-permute-start
  110.8 3.5 collective-permute-start.1
  114.3 1.2 copy-start.27
  115.5 45.8 %copy-start.6 = (bf16[2,128,1280]{2,1,0:T(8,128)(2,1)S(1)}, bf16[2,128,1280]{2,1,0:T(8,128)(2,1)}, u32[]{:S(2)}) copy-start(bf16[2,128,1280]{2,1,0:T(8,128)(2,1)} %param.10) | copy-start | bytes 1966084
  145.8 15.5 %all-to-all-start = ((bf16[16,80,256]{2,1,0:T(8,128)(2,1)}), bf16[16,80,256]{2,1,0:T(8,128)(2,1)S(1)}, u32[]{:S(2)}, u32[]{:S(2)}) async-start(bf16[16,80,256]{2,1,0:T(8,128)(2,1)} %get-tuple-element.36), calls=%async_computation | async-start | bytes 1310720 | tf_op jit(solution)/shard_map/all_to_all | solution.py:316
  151.7 202.3 %reduce-scatter.4.cloned.1.call-start = ((), (), s32[]{:S(2)}) async-start(), calls=%async_computation.12 | async-start | bytes 6144000 | tf_op jit(solution)/shard_map/reduce_scatter | solution.py:401
  161.3 3.4 copy-start.3
  164.9 17.6 %copy-start.8 = (bf16[2,128,1280]{2,1,0:T(8,128)(2,1)S(1)}, bf16[2,128,1280]{2,1,0:T(8,128)(2,1)}, u32[]{:S(2)}) copy-start(bf16[2,128,1280]{2,1,0:T(8,128)(2,1)} %param.12) | copy-start | bytes 1966084
  182.5 3.6 copy-start.11
  186.1 5.8 %copy-start.15 = (bf16[256,1280]{0,1:T(8,128)(2,1)}, bf16[256,1280]{0,1:T(8,128)(2,1)S(1)}, u32[]{:S(2)}) copy-start(bf16[256,1280]{0,1:T(8,128)(2,1)S(1)} %fusion.2) | copy-start | bytes 1966084
  186.1 1.3 copy-start.9
  187.4 1.9 copy-start.26
  189.3 3.2 copy-start.13
  189.3 1.9 copy-start.12
  196.1 8.5 %collective-permute-start.11 = (bf16[1280,1920]{0,1:T(8,128)(2,1)}, bf16[1280,1920]{0,1:T(8,128)(2,1)}, u32[]{:S(2)}, u32[]{:S(2)}) collective-permute-start(bf16[1280,1920]{0,1:T(8,128)(2,1)} %pad_maximum_fusion), channel_id=1, source_target_pairs={{0,4},{4,0},{1,5},{5,1},{2,6},{6,2},{3,7},{7,3},{8,12},{12,8},{9,1... | collective-permute-start | bytes 14745608 | tf_op jit(solution)/shard_map/ppermute | solution.py:292
  196.4 1.9 copy-start.16
  198.2 1.3 copy-start.14
  217.1 192.9 %all-gather.14.cloned.1.call-start = ((), (), s32[]{:S(2)}) async-start(), calls=%async_computation.11 | async-start | bytes 11059200 | tf_op jit(solution)/shard_map/all_gather | solution.py:312
  219.6 8.0 %collective-permute-start.2 = (bf16[2,2048,128]{2,1,0:T(8,128)(2,1)}, bf16[2,2048,128]{2,1,0:T(8,128)(2,1)}, u32[]{:S(2)}, u32[]{:S(2)}) collective-permute-start(bf16[2,2048,128]{2,1,0:T(8,128)(2,1)} %get-tuple-element.39.vo_ref), channel_id=1, source_target_pairs={{0,4},{4,0},{1,5},{5,1},{2,6},{6,2},{3,7},{7,3},{8,12},{12,8},{9,1... | collective-permute-start | bytes 3145736 | tf_op jit(solution)/shard_map/ppermute | solution.py:292
  219.9 7.7 %collective-permute-start.3 = (bf16[2,80,2048]{2,1,0:T(8,128)(2,1)}, bf16[2,80,2048]{2,1,0:T(8,128)(2,1)}, u32[]{:S(2)}, u32[]{:S(2)}) collective-permute-start(bf16[2,80,2048]{2,1,0:T(8,128)(2,1)} %get-tuple-element.40.kto_ref), channel_id=1, source_target_pairs={{0,4},{4,0},{1,5},{5,1},{2,6},{6,2},{3,7},{7,3},{8,12},{12,8},{9,1... | collective-permute-start | bytes 1966088 | tf_op jit(solution)/shard_map/ppermute | solution.py:292
  220.2 18.6 %all-to-all-start.1 = ((bf16[16,80,256]{2,1,0:T(8,128)(2,1)}), bf16[16,80,256]{2,1,0:T(8,128)(2,1)S(1)}, u32[]{:S(2)}, u32[]{:S(2)}) async-start(bf16[16,80,256]{2,1,0:T(8,128)(2,1)} %bitcast.8), calls=%async_computation.1 | async-start | bytes 1310720 | tf_op jit(solution)/shard_map/all_to_all | solution.py:316
  282.0 3.0 collective-permute-start.4
  282.0 6.0 %collective-permute-start.5 = (bf16[2,2048,128]{2,1,0:T(8,128)(2,1)}, bf16[2,2048,128]{2,1,0:T(8,128)(2,1)}, u32[]{:S(2)}, u32[]{:S(2)}) collective-permute-start(bf16[2,2048,128]{2,1,0:T(8,128)(2,1)} %get-tuple-element.48), channel_id=1, source_target_pairs={{0,4},{4,0},{1,5},{5,1},{2,6},{6,2},{3,7},{7,3},{8,12},{12,8},{9,1... | collective-permute-start | bytes 3145736 | tf_op jit(solution)/shard_map/ppermute | solution.py:292
  288.0 17.7 %copy-start.21 = (f32[80,256]{1,0:T(8,128)S(1)}, f32[80,256]{1,0:T(8,128)}, u32[]{:S(2)}) copy-start(f32[80,256]{1,0:T(8,128)} %get-tuple-element.52) | copy-start | bytes 245764
  305.5 1.7 collective-permute-start.6
  309.1 8.9 %collective-permute-start.9 = (bf16[168,256]{1,0:T(8,128)(2,1)}, bf16[168,256]{1,0:T(8,128)(2,1)S(1)}, u32[]{:S(2)}, u32[]{:S(2)}) collective-permute-start(bf16[168,256]{1,0:T(8,128)(2,1)} %get-tuple-element.79), channel_id=1, source_target_pairs={{0,2},{1,3},{2,0},{3,1},{4,6},{5,7},{6,4},{7,5},{8,10},{9,11},{10,... | collective-permute-start | bytes 258056 | tf_op jit(solution)/shard_map/ppermute | solution.py:301
  312.0 9.4 %collective-permute-start.8 = (bf16[168,256]{1,0:T(8,128)(2,1)}, bf16[168,256]{1,0:T(8,128)(2,1)}, u32[]{:S(2)}, u32[]{:S(2)}) collective-permute-start(bf16[168,256]{1,0:T(8,128)(2,1)} %get-tuple-element.80), channel_id=1, source_target_pairs={{0,3},{1,0},{2,1},{3,2},{4,7},{5,4},{6,5},{7,6},{8,11},{9,8},{10,9... | collective-permute-start | bytes 258056 | tf_op jit(solution)/shard_map/ppermute | solution.py:301
  314.2 8.2 %collective-permute-start.7 = (bf16[168,256]{1,0:T(8,128)(2,1)S(1)}, bf16[168,256]{1,0:T(8,128)(2,1)}, u32[]{:S(2)}, u32[]{:S(2)}) collective-permute-start(bf16[168,256]{1,0:T(8,128)(2,1)S(1)} %get-tuple-element.78), channel_id=1, source_target_pairs={{0,1},{1,2},{2,3},{3,0},{4,5},{5,6},{6,7},{7,4},{8,9},{9,10},{10,1... | collective-permute-start | bytes 258056 | tf_op jit(solution)/shard_map/ppermute | solution.py:301
  347.6 29.4 %all-to-all-start.2 = ((bf16[16,240,256]{2,1,0:T(8,128)(2,1)}), bf16[16,240,256]{2,1,0:T(8,128)(2,1)}, u32[]{:S(2)}, u32[]{:S(2)}) async-start(bf16[16,240,256]{2,1,0:T(8,128)(2,1)} %get-tuple-element.50), calls=%async_computation.2 | async-start | bytes 3932160 | tf_op jit(solution)/shard_map/all_to_all | solution.py:316
  356.3 27.8 %copy-start.7 = (bf16[2,128,1280]{2,1,0:T(8,128)(2,1)S(1)}, bf16[2,128,1280]{2,1,0:T(8,128)(2,1)}, u32[]{:S(2)}) copy-start(bf16[2,128,1280]{2,1,0:T(8,128)(2,1)} %param.10) | copy-start | bytes 1966084
  377.0 23.4 %all-to-all-start.4 = ((bf16[16,20,1920]{2,1,0:T(8,128)(2,1)}), bf16[16,20,1920]{2,1,0:T(8,128)(2,1)}, u32[]{:S(2)}, u32[]{:S(2)}) async-start(bf16[16,20,1920]{2,1,0:T(8,128)(2,1)} %reshape.309), calls=%async_computation.4 | async-start | bytes 2949120 | tf_op jit(solution)/shard_map/all_to_all | solution.py:316
  388.3 44.5 %collective-permute-start.10 = (bf16[16,168,256]{2,1,0:T(8,128)(2,1)}, bf16[16,168,256]{2,1,0:T(8,128)(2,1)}, u32[]{:S(2)}, u32[]{:S(2)}) collective-permute-start(bf16[16,168,256]{2,1,0:T(8,128)(2,1)} %all_to_all.30), channel_id=1, source_target_pairs={{0,4},{4,0},{1,5},{5,1},{2,6},{6,2},{3,7},{7,3},{8,12},{12,8},{9,1... | collective-permute-start | bytes 4128776 | tf_op jit(solution)/shard_map/ppermute | solution.py:292
  403.2 23.9 %all-to-all-start.5 = ((bf16[16,20,1920]{2,1,0:T(8,128)(2,1)}), bf16[16,20,1920]{2,1,0:T(8,128)(2,1)}, u32[]{:S(2)}, u32[]{:S(2)}) async-start(bf16[16,20,1920]{2,1,0:T(8,128)(2,1)} %broadcast_in_dim.80), calls=%async_computation.5 | async-start | bytes 2949120 | tf_op jit(solution)/shard_map/all_to_all | solution.py:316
  429.4 17.1 %collective-permute-start.12 = (bf16[320,1920]{1,0:T(8,128)(2,1)}, bf16[320,1920]{1,0:T(8,128)(2,1)S(1)}, u32[]{:S(2)}, u32[]{:S(2)}) collective-permute-start(bf16[320,1920]{1,0:T(8,128)(2,1)} %reshape.310), channel_id=1, source_target_pairs={{0,4},{4,0},{1,5},{5,1},{2,6},{6,2},{3,7},{7,3},{8,12},{12,8},{9,1... | collective-permute-start | bytes 3686408 | tf_op jit(solution)/shard_map/ppermute | solution.py:292
  436.2 5.4 %copy-start.2 = (bf16[320,3840]{1,0:T(8,128)(2,1)S(1)}, bf16[320,3840]{1,0:T(8,128)(2,1)}, u32[]{:S(2)}) copy-start(bf16[320,3840]{1,0:T(8,128)(2,1)} %param.13) | copy-start | bytes 7372804
  441.6 4.9 %copy-start.10 = (bf16[320,1920]{1,0:T(8,128)(2,1)S(1)}, bf16[320,1920]{1,0:T(8,128)(2,1)}, u32[]{:S(2)}) copy-start(bf16[320,1920]{1,0:T(8,128)(2,1)} %reshape.310) | copy-start | bytes 3686404
  449.9 2.5 copy-start.1
  (5 other events, 5.0 us)
Sparse Core Ops, SparseCore 0:
  10.2 82.9 all-gather.5
  94.9 27.8 all-gather.7
  124.5 28.2 all-gather.11
  154.3 28.1 all-gather.9
  217.2 52.5 reduce-scatter.3
  272.1 59.1 all-gather.13
